TPU v7x, 1024 devices: a whole 4x4x32 slice. The times are simulated.
1024 devices in a mesh: dp: 32 (over x, y, core), tensor: 32 (over z).
Axes of the slice: x: 4, y: 4, z: 32, core: 2. Of those that a mesh axis runs over, the one named last changes fastest.
Arguments:
- gradients: float32 [32, 128, 28672], P('dp', None, 'tensor'), may hold values from -110 to 110
- error_memory: bfloat16 [32, 128, 28672], P('dp', None, 'tensor'), may hold values from -2 to 2
- q_start: float32 [28672, 32], P('tensor'), may hold values from -5 to 5
Outputs:
- p_factor: float32 [128, 32], P('tensor')
- q_factor: float32 [28672, 32], P('tensor')
- new_error: bfloat16 [32, 128, 28672], P('dp', None, 'tensor')
All inputs are finite; a program needn't handle non-finite values.
Results may differ from a plain program's by a relative error of at most 0.0019.
Values sent between devices are 32-bit elements; how exact they have to be, the bound alone decides.
A program may use at most 32 MiB of HBM per device.

v0:
```python
import jax
import jax.numpy as jnp
from jax import lax
from jax.sharding import PartitionSpec as P

ITERS = 2


def orthonormal_local(p_sum, gram):
    chol = jnp.linalg.cholesky(gram)
    return jax.scipy.linalg.solve_triangular(chol, p_sum.T, lower=True).T


def inner_rows(left, right):
    return lax.dot_general(
        left,
        right,
        (((0,), (0,)), ((), ())),
        precision=lax.Precision.HIGHEST,
        preferred_element_type=jnp.float32,
    )


def local(gradients, error_memory, q_start):
    corrected = gradients[0] + error_memory[0].astype(jnp.float32)
    rows_total = corrected.shape[0]
    rows_mine = rows_total // lax.axis_size("tensor")
    replica_count = lax.axis_size("dp")
    q_now = q_start
    own_orth = jnp.zeros((rows_mine, q_start.shape[1]), jnp.float32)
    full_orth = jnp.zeros((rows_total, q_start.shape[1]), jnp.float32)
    for step in range(ITERS):
        term = jnp.dot(
            corrected, q_now, precision=lax.Precision.HIGHEST, preferred_element_type=jnp.float32
        )
        replica_sum = lax.psum(term, "dp")
        own_sum = lax.psum_scatter(replica_sum, "tensor", scatter_dimension=0, tiled=True)
        gram = lax.psum(inner_rows(own_sum, own_sum), "tensor")
        own_orth = orthonormal_local(own_sum, gram)
        full_orth = lax.all_gather(own_orth, "tensor", axis=0, tiled=True)
        q_term = inner_rows(corrected, full_orth)
        q_now = lax.psum(q_term, "dp") / replica_count
    product = lax.dot_general(
        full_orth,
        q_now,
        (((1,), (1,)), ((), ())),
        precision=lax.Precision.HIGHEST,
        preferred_element_type=jnp.float32,
    )
    new_error = (corrected - product).astype(jnp.bfloat16)[None]
    return (own_orth, q_now, new_error)


def solution(mesh):
    in_specs = (P("dp", None, "tensor"), P("dp", None, "tensor"), P("tensor", None))
    out_specs = (P("tensor", None), P("tensor", None), P("dp", None, "tensor"))
    return jax.shard_map(local, mesh=mesh, in_specs=in_specs, out_specs=out_specs, check_vma=False)
```

profile of v0, /device:TPU:1, one launch (start us, length us, event | category | flops | bytes accessed | tf_op | source)
XLA Modules:
  0.0 1028.3 jit_solution(7747344679772869553)
XLA Ops:
  7.2 0.0 copy-start
  7.2 0.0 all-reduce.5.cloned.1.call-start
  7.2 0.8 copy-done
  8.1 0.0 copy-start.2
  8.1 1.6 fusion.8
  9.7 0.0 copy-start.1
  9.7 94.5 %all-reduce = f32[128,32]{1,0:T(8,128)S(1)} all-reduce(f32[128,32]{1,0:T(8,128)S(1)} %fusion.8), channel_id=2, replica_groups=mesh['dp'=32,'tensor'=32] {'tensor'}, use_global_device_ids=true, to_apply=%region_1.0.clone | all-reduce | flops 4096 | bytes 32768
  104.3 1.3 dynamic-slice
  106.2 90.1 %psum.48 = f32[4,32]{1,0:T(4,128)S(1)} all-reduce(f32[4,32]{1,0:T(4,128)S(1)} %constant_dynamic-slice_fusion.1), channel_id=1, replica_groups=mesh['dp'=32,'tensor'=32] {'dp'}, use_global_device_ids=true, to_apply=%region_0.0 | all-reduce | flops 128 | bytes 1024 | tf_op jit(solution)/shard_map/psum | solution.py:36
  196.3 0.2 fusion.24
  196.5 76.7 %psum.43 = f32[32,32]{0,1:T(8,128)S(1)} all-reduce(f32[32,32]{0,1:T(8,128)S(1)} %fusion.24), channel_id=1, replica_groups=mesh['dp'=32,'tensor'=32] {'tensor'}, use_global_device_ids=true, to_apply=%region_2.0 | all-reduce | flops 1024 | bytes 8192 | tf_op jit(solution)/shard_map/psum | solution.py:38
  273.2 0.1 copy.11
  273.3 2.9 cholesky.44
  276.2 0.6 compare_reduce_fusion.1
  276.8 0.7 fusion.12
  277.5 2.4 custom-call.6
  279.9 0.2 convolution_bitcast_fusion
  280.1 38.1 %all-gather = f32[32,4,32]{2,1,0:T(4,128)S(1)} all-gather(f32[1,4,32]{2,1,0:T(4,128)S(1)} %convolution_bitcast_fusion), channel_id=1, replica_groups=mesh['dp'=32,'tensor'=32] {'tensor'}, dimensions={0}, use_global_device_ids=true | all-gather | bytes 16896 | tf_op jit(solution)/shard_map/all_gather | solution.py:40
  318.2 0.0 copy-done.2
  318.3 0.0 copy-done.1
  318.3 1.1 fusion.6
  319.3 0.0 all-reduce.5.cloned.1.call-update
  319.3 0.0 all-reduce.7.cloned.1.call-start
  319.4 199.3 %all-reduce.5.cloned.1.call-done = f32[896,32]{0,1:T(8,128)} async-done(((f32[896,32]{0,1:T(8,128)}), f32[896,32]{0,1:T(8,128)}) %all-reduce.5.cloned.1.call-update) | async-done | bytes 114704 | tf_op jit(solution)/shard_map/psum | solution.py:42
  518.7 1.4 fusion.4
  520.1 83.6 %all-reduce.1 = f32[128,32]{1,0:T(8,128)S(1)} all-reduce(f32[128,32]{1,0:T(8,128)S(1)} %fusion.4), channel_id=3, replica_groups=mesh['dp'=32,'tensor'=32] {'tensor'}, use_global_device_ids=true, to_apply=%region_7.0.clone | all-reduce | flops 4096 | bytes 32768
  603.7 88.6 %psum.49 = f32[4,32]{1,0:T(4,128)S(1)} all-reduce(f32[4,32]{1,0:T(4,128)S(1)} %constant_dynamic-slice_fusion), channel_id=1, replica_groups=mesh['dp'=32,'tensor'=32] {'dp'}, use_global_device_ids=true, to_apply=%region_6.0 | all-reduce | flops 128 | bytes 1024 | tf_op jit(solution)/shard_map/psum | solution.py:36
  692.2 0.2 fusion.25
  692.5 78.2 %psum.46 = f32[32,32]{0,1:T(8,128)S(1)} all-reduce(f32[32,32]{0,1:T(8,128)S(1)} %fusion.25), channel_id=1, replica_groups=mesh['dp'=32,'tensor'=32] {'tensor'}, use_global_device_ids=true, to_apply=%region_8.11 | all-reduce | flops 1024 | bytes 8192 | tf_op jit(solution)/shard_map/psum | solution.py:38
  770.7 0.1 copy.13
  770.8 2.9 cholesky.55
  773.7 0.6 compare_reduce_fusion
  774.4 0.7 fusion.13
  775.0 2.4 custom-call.7
  777.4 0.2 fusion.14
  777.6 0.0 copy-start.4
  777.6 40.0 %all-gather.1 = f32[32,4,32]{2,1,0:T(4,128)S(1)} all-gather(f32[1,4,32]{2,1,0:T(4,128)S(1)} %bitcast.58), channel_id=1, replica_groups=mesh['dp'=32,'tensor'=32] {'tensor'}, dimensions={0}, use_global_device_ids=true | all-gather | bytes 16896 | tf_op jit(solution)/shard_map/all_gather | solution.py:40
  817.6 0.0 copy-done.4
  817.6 1.1 fusion.2
  818.6 0.0 all-reduce.7.cloned.1.call-update
  818.7 200.6 %all-reduce.7.cloned.1.call-done = f32[896,32]{0,1:T(8,128)} async-done(((f32[896,32]{0,1:T(8,128)}), f32[896,32]{0,1:T(8,128)}) %all-reduce.7.cloned.1.call-update) | async-done | bytes 114704 | tf_op jit(solution)/shard_map/psum | solution.py:42
  1019.3 0.9 broadcast_multiply_fusion
  1020.2 0.0 copy-start.3
  1020.2 1.2 fusion.1
  1021.4 0.0 copy-done.3
  (6 shorter events, 0.1 us)
Async XLA Ops:
  7.2 0.9 copy-start
  7.2 511.5 %all-reduce.5.cloned.1.call-start = ((), (), s32[]{:S(2)}) async-start(), calls=%async_computation | async-start | bytes 229376 | tf_op jit(solution)/shard_map/psum | solution.py:42
  8.1 310.2 %copy-start.2 = (bf16[1,128,896]{2,1,0:T(8,128)(2,1)S(1)}, bf16[1,128,896]{2,1,0:T(8,128)(2,1)}, u32[]{:S(2)}) copy-start(bf16[1,128,896]{2,1,0:T(8,128)(2,1)} %param.7) | copy-start | bytes 688132
  9.7 308.6 %copy-start.1 = (f32[1,128,896]{2,1,0:T(8,128)S(1)}, f32[1,128,896]{2,1,0:T(8,128)}, u32[]{:S(2)}) copy-start(f32[1,128,896]{2,1,0:T(8,128)} %param.6) | copy-start | bytes 1376260
  319.3 699.9 %all-reduce.7.cloned.1.call-start = ((), (), s32[]{:S(2)}) async-start(), calls=%async_computation.1 | async-start | bytes 229376 | tf_op jit(solution)/shard_map/psum | solution.py:42
  777.6 40.0 %copy-start.4 = (f32[32,4]{0,1:T(4,128)}, f32[32,4]{0,1:T(4,128)S(1)}, u32[]{:S(2)}) copy-start(f32[32,4]{0,1:T(4,128)S(1)} %fusion.14) | copy-start | bytes 1540
  1020.2 1.2 copy-start.3
Sparse Core Ops, SparseCore 0:
  319.5 199.1 all-reduce.4
  818.8 200.4 all-reduce.6
where the time goes:
time: 1030 us
  blocking collectives  590 us (57%)
  waiting for transfers between devices  400 us (39%)
  between operations  14.8 us (1%)
  other arithmetic  14.3 us (1%)
    psum x2, waiting for transfers between devices, local(): q_now = lax.psum(q_term, 'dp') / replica_count  400 us
    psum x2, blocking collectives, local(): replica_sum = lax.psum(term, 'dp')  179 us
    unnamed x2, blocking collectives  178 us
    psum x2, blocking collectives, local(): gram = lax.psum(inner_rows(own_sum, own_sum), 'tensor')  155 us
    all_gather x2, blocking collectives, local(): full_orth = lax.all_gather(own_orth, 'tensor', axis=0, tiled=True)  78.1 us
  transfers between devices with their start and end apart: 2, of which 2 were waited for; matrix products, arithmetic and copies ran while one was open for 0% of the time, Pallas kernels for 0%

commit v1 on v0

v1 whole, which is shorter than its diff:
```python
import jax
import jax.numpy as jnp
from jax import lax
from jax.experimental import pallas as pl
from jax.experimental.pallas import tpu as pltpu
from jax.sharding import PartitionSpec as P

MESH = pl.DeviceIdType.MESH
HIGH = lax.Precision.HIGHEST
ROWS = 128
COLS = 896
HALF = 448
RANK = 32
CHIPS = 16
OWNERS = 14
SLICE = 32
SOURCES = 2 * OWNERS
DEPTH = 32
PLANE = 32


def dot(left, right, left_dim, right_dim):
    return lax.dot_general(
        left,
        right,
        (((left_dim,), (right_dim,)), ((), ())),
        precision=HIGH,
        preferred_element_type=jnp.float32,
    )


def wait_bytes(ref, sem):
    pltpu.make_async_copy(ref, ref, sem).wait()


def reduce_kernel(
    g_hbm, e_hbm, q_hbm, m_out, st_out,
    g_v, e_v, q_v, ct, sib, rs, part, tiles, zb,
    load_sem, sib_sem, rs_sem, tile_sem, z_sem, m_sem, st_sem, go_sem,
):
    dp = lax.axis_index("dp")
    z = lax.axis_index("tensor")
    core = lax.rem(dp, 2)
    chip = lax.div(dp, 2)

    loads = [
        pltpu.make_async_copy(g_hbm.at[0], g_v, load_sem.at[0]),
        pltpu.make_async_copy(e_hbm.at[0], e_v, load_sem.at[1]),
        pltpu.make_async_copy(q_hbm, q_v, load_sem.at[2]),
    ]
    for load in loads:
        load.start()

    barrier = pltpu.get_barrier_semaphore()

    @pl.loop(0, CHIPS)
    def _(j):
        @pl.when(2 * j != dp)
        def _():
            pl.semaphore_signal(barrier, inc=1, device_id=(2 * j, z), device_id_type=MESH)

    @pl.when(core == 1)
    def _():
        @pl.loop(1, DEPTH)
        def _(k):
            pl.semaphore_signal(
                barrier, inc=1, device_id=(dp, lax.rem(z + k, DEPTH)), device_id_type=MESH
            )

    for load in loads:
        load.wait()
    for b in range(COLS // 128):
        cols = slice(128 * b, 128 * b + 128)
        ct[cols, :] = (g_v[:, cols] + e_v[:, cols].astype(jnp.float32)).T

    @pl.when(core == 0)
    def _():
        pl.semaphore_wait(barrier, PLANE - 1)
        pl.semaphore_signal(go_sem, inc=1, device_id=(dp + 1, z), device_id_type=MESH)

    @pl.when(core == 1)
    def _():
        pl.semaphore_wait(go_sem, 1)

    mine = pl.multiple_of(core * HALF, 8)
    other = pl.multiple_of((1 - core) * HALF, 8)
    swap = pltpu.make_async_remote_copy(
        src_ref=ct.at[pl.ds(other, HALF)], dst_ref=sib, send_sem=sib_sem.at[0], recv_sem=sib_sem.at[1],
        device_id=(dp + 1 - 2 * core, z), device_id_type=MESH,
    )
    swap.start()
    swap.wait_recv()
    ct[pl.ds(mine, HALF), :] += sib[...]

    @pl.loop(0, OWNERS)
    def _(j):
        @pl.when(j != chip)
        def _():
            pltpu.make_async_remote_copy(
                src_ref=ct.at[pl.ds(pl.multiple_of(mine + SLICE * j, 8), SLICE)], dst_ref=rs.at[chip],
                send_sem=rs_sem.at[0], recv_sem=rs_sem.at[1],
                device_id=(2 * j + core, z), device_id_type=MESH,
            ).start()

    own = pl.multiple_of(mine + SLICE * lax.min(chip, OWNERS - 1), 8)
    source = core * OWNERS + lax.min(chip, OWNERS - 1)

    @pl.when(chip < OWNERS)
    def _():
        rs[chip] = ct[pl.ds(own, SLICE), :]
        wait_bytes(rs.at[pl.ds(0, CHIPS - 1)], rs_sem.at[1])
        total = rs[0]
        for j in range(1, CHIPS):
            total += rs[j]
        st_out[pl.ds(own, SLICE), :] = total
        gram = dot(total, total, 0, 0)
        left = dot(q_v[pl.ds(own, SLICE), :], total, 0, 0)
        for t in range(4):
            part[t] = left[8 * t : 8 * t + 8]
        for t in range(8):
            part[4 + t] = gram[8 * t : 8 * t + 8]
        upper = gram[64:96, :]
        lower = pltpu.roll(gram[96:128, :], 64, 1)
        lane = lax.broadcasted_iota(jnp.int32, (32, 128), 1)
        packed = jnp.where(lane < 64, lower, upper)
        for t in range(4):
            part[12 + t] = packed[8 * t : 8 * t + 8]

        @pl.loop(0, CHIPS)
        def _(j):
            @pl.when(2 * j + 1 != dp)
            def _():
                pltpu.make_async_remote_copy(
                    src_ref=part.at[j], dst_ref=tiles.at[source], send_sem=tile_sem.at[0], recv_sem=tile_sem.at[1],
                    device_id=(2 * j + 1, z), device_id_type=MESH,
                ).start()

    @pl.when(core == 1)
    def _():
        @pl.when(chip < OWNERS)
        def _():
            tiles[source] = part[chip]
            wait_bytes(tiles.at[pl.ds(0, SOURCES - 1)], tile_sem.at[1])

        @pl.when(chip >= OWNERS)
        def _():
            wait_bytes(tiles, tile_sem.at[1])

        total = tiles[0]
        for j in range(1, SOURCES):
            total += tiles[j]
        zb[z] = total
        pl.semaphore_wait(barrier, DEPTH - 1)

        @pl.loop(0, DEPTH - 1)
        def _(k):
            half = lax.div(k + 1, 2)
            shift = jnp.where(lax.rem(k, 2) == 0, 16 + half, 16 - half)
            pltpu.make_async_remote_copy(
                src_ref=zb.at[z], dst_ref=zb.at[z], send_sem=z_sem.at[0], recv_sem=z_sem.at[1],
                device_id=(dp, lax.rem(z + shift, DEPTH)), device_id_type=MESH,
            ).start()

    @pl.when(chip < OWNERS)
    def _():
        @pl.loop(1, PLANE)
        def _(k):
            pltpu.make_async_remote_copy(
                src_ref=st_out.at[pl.ds(own, SLICE)], dst_ref=st_out.at[pl.ds(own, SLICE)],
                send_sem=st_sem.at[0], recv_sem=st_sem.at[1],
                device_id=(lax.rem(dp + k, PLANE), z), device_id_type=MESH,
            ).start()

    @pl.when(core == 1)
    def _():
        wait_bytes(zb.at[pl.ds(0, DEPTH - 1)], z_sem.at[1])
        total = zb[0]
        for j in range(1, DEPTH):
            total += zb[j]
        m_out[chip] = total

        @pl.loop(1, PLANE)
        def _(k):
            pltpu.make_async_remote_copy(
                src_ref=m_out.at[chip], dst_ref=m_out.at[chip], send_sem=m_sem.at[0], recv_sem=m_sem.at[1],
                device_id=(lax.rem(dp + k, PLANE), z), device_id_type=MESH,
            ).start()
        wait_bytes(m_out.at[pl.ds(0, CHIPS - 1)], m_sem.at[1])
        wait_bytes(zb.at[pl.ds(0, DEPTH - 1)], z_sem.at[0])
        wait_bytes(zb.at[pl.ds(0, PLANE - 1)], m_sem.at[0])

    @pl.when(core == 0)
    def _():
        wait_bytes(m_out, m_sem.at[1])

    swap.wait_send()

    @pl.when(chip < OWNERS)
    def _():
        wait_bytes(st_out.at[pl.ds(0, COLS - SLICE)], st_sem.at[1])
        wait_bytes(ct.at[pl.ds(0, SLICE * (OWNERS - 1))], rs_sem.at[0])
        wait_bytes(st_out, st_sem.at[0])
        wait_bytes(st_out.at[pl.ds(0, COLS // 28 * 3)], st_sem.at[0])

        @pl.when(core == 0)
        def _():
            wait_bytes(part, tile_sem.at[0])

        @pl.when(core == 1)
        def _():
            wait_bytes(part.at[pl.ds(0, CHIPS - 1)], tile_sem.at[0])

    @pl.when(chip >= OWNERS)
    def _():
        wait_bytes(st_out, st_sem.at[1])
        wait_bytes(ct.at[pl.ds(0, HALF)], rs_sem.at[0])


def reduce_call(gradients, error_memory, q_start):
    any_space = pl.BlockSpec(memory_space=pl.ANY)
    vmem = pl.BlockSpec(memory_space=pltpu.VMEM)
    pair = pltpu.SemaphoreType.DMA((2,))
    return pl.pallas_call(
        reduce_kernel,
        out_shape=(
            jax.ShapeDtypeStruct((CHIPS, 8, 128), jnp.float32),
            jax.ShapeDtypeStruct((COLS, ROWS), jnp.float32),
        ),
        in_specs=[any_space] * 3,
        out_specs=(vmem, vmem),
        scratch_shapes=[
            pltpu.VMEM((ROWS, COLS), jnp.float32),
            pltpu.VMEM((ROWS, COLS), jnp.bfloat16),
            pltpu.VMEM((COLS, RANK), jnp.float32),
            pltpu.VMEM((COLS, ROWS), jnp.float32),
            pltpu.VMEM((HALF, ROWS), jnp.float32),
            pltpu.VMEM((CHIPS, SLICE, ROWS), jnp.float32),
            pltpu.VMEM((CHIPS, 8, 128), jnp.float32),
            pltpu.VMEM((SOURCES, 8, 128), jnp.float32),
            pltpu.VMEM((DEPTH, 8, 128), jnp.float32),
            pltpu.SemaphoreType.DMA((3,)),
            pair, pair, pair, pair, pair, pair,
            pltpu.SemaphoreType.REGULAR,
        ],
        compiler_params=pltpu.CompilerParams(
            collective_id=0, has_side_effects=True, vmem_limit_bytes=16 << 20
        ),
        name="plane_and_line_sums",
    )(gradients, error_memory, q_start)


def orthonormal_rows(pt):
    gram = dot(pt, pt, 1, 1)
    row = lax.broadcasted_iota(jnp.int32, (RANK, 1), 0)
    for k in range(RANK):
        pivot = gram[k : k + 1, k : k + 1]
        factor = jnp.where(row > k, gram[:, k : k + 1] / pivot, 0.0)
        gram, pt = gram - factor * gram[k : k + 1, :], pt - factor * pt[k : k + 1, :]
    diag = lax.broadcasted_iota(jnp.int32, (RANK, RANK), 0) == lax.broadcasted_iota(jnp.int32, (RANK, RANK), 1)
    pivots = jnp.sum(jnp.where(diag, gram, 0.0), axis=1, keepdims=True)
    return pt / jnp.sqrt(pivots)


def factor_kernel(m_ref, st_ref, g_hbm, e_hbm, p_out, q_out, new_out, g_v, e_v, load_sem):
    loads = [
        pltpu.make_async_copy(g_hbm.at[0], g_v, load_sem.at[0]),
        pltpu.make_async_copy(e_hbm.at[0], e_v, load_sem.at[1]),
    ]
    for load in loads:
        load.start()
    pt = jnp.concatenate([m_ref[t] for t in range(4)], axis=0)
    top = jnp.concatenate([m_ref[4 + t] for t in range(8)], axis=0)
    packed = jnp.concatenate([m_ref[12 + t] for t in range(4)], axis=0)
    lane = lax.broadcasted_iota(jnp.int32, (64, 128), 1)
    right = jnp.concatenate([packed, pltpu.roll(packed, 64, 1)], axis=0)
    wide = jnp.concatenate([top, top], axis=0).T
    bottom = jnp.where(lane < 64, wide[64:128, :], right)
    gram = jnp.concatenate([top, bottom], axis=0)

    first = orthonormal_rows(pt)
    second = dot(first, gram, 1, 0) * (1.0 / REPLICAS)
    pt = orthonormal_rows(second)

    z = lax.axis_index("tensor")
    pick = lax.broadcasted_iota(jnp.int32, (8, ROWS), 0) + 4 * z == lax.broadcasted_iota(jnp.int32, (8, ROWS), 1)
    p_out[...] = dot(pick.astype(jnp.float32), pt, 1, 1)[0:4, :]
    st = st_ref[...]
    q_out[...] = dot(st, pt, 1, 1) * (1.0 / REPLICAS)
    qt = dot(pt, st, 1, 1) * (1.0 / REPLICAS)
    product = dot(pt, qt, 0, 0)
    for load in loads:
        load.wait()
    new_out[0] = (g_v[...] + e_v[...].astype(jnp.float32) - product).astype(jnp.bfloat16)


REPLICAS = 32


def factor_call(tiles, st, gradients, error_memory):
    any_space = pl.BlockSpec(memory_space=pl.ANY)
    vmem = pl.BlockSpec(memory_space=pltpu.VMEM)
    return pl.pallas_call(
        factor_kernel,
        out_shape=(
            jax.ShapeDtypeStruct((4, RANK), jnp.float32),
            jax.ShapeDtypeStruct((COLS, RANK), jnp.float32),
            jax.ShapeDtypeStruct((1, ROWS, COLS), jnp.bfloat16),
        ),
        in_specs=[vmem, vmem, any_space, any_space],
        out_specs=(vmem, vmem, vmem),
        scratch_shapes=[
            pltpu.VMEM((ROWS, COLS), jnp.float32),
            pltpu.VMEM((ROWS, COLS), jnp.bfloat16),
            pltpu.SemaphoreType.DMA((2,)),
        ],
        compiler_params=pltpu.CompilerParams(vmem_limit_bytes=16 << 20),
        name="factors",
    )(tiles, st, gradients, error_memory)


def local(gradients, error_memory, q_start):
    tiles, st = reduce_call(gradients, error_memory, q_start)
    return factor_call(tiles, st, gradients, error_memory)


def solution(mesh):
    in_specs = (P("dp", None, "tensor"), P("dp", None, "tensor"), P("tensor", None))
    out_specs = (P("tensor", None), P("tensor", None), P("dp", None, "tensor"))
    return jax.shard_map(local, mesh=mesh, in_specs=in_specs, out_specs=out_specs, check_vma=False)
```

time: 1030 us -> 66.6 us (0.06)
  blocking collectives: 590 us -> 0 us
  waiting for transfers between devices: 400 us -> 0 us
  Pallas kernels: 0 us -> 62.8 us
  other arithmetic: 14.3 us -> 0 us
  between operations: 14.8 us -> 0.68 us
    psum x2 -> x0, waiting for transfers between devices: 400 us -> none  [local(): q_now = lax.psum(q_term, 'dp') / replica_count]
    psum x4 -> x0, blocking collectives: 334 us -> none  [the longest x2 179 us: local(): replica_sum = lax.psum(term, 'dp')]
    unnamed x2 -> x0, blocking collectives: 178 us -> none
    all_gather x2 -> x0, blocking collectives: 78.1 us -> none  [local(): full_orth = lax.all_gather(own_orth, 'tensor', axis=0, tiled=True)]
    pallas_call x0 -> x2, Pallas kernels: none -> 62.8 us  [the longest x1 54.3 us: reduce_call(): pl.pallas_call(reduce_kernel, out_shape=(jax.ShapeDtypeStruct((CHIPS, 8,...]
    another operation x10 -> x0, other arithmetic: 13.4 us -> none  [the longest x6 7.19 us: orthonormal_local(): chol = jnp.linalg.cholesky(gram)]
  transfers between devices with their start and end apart: 2 -> 0, of which waited for: 2 -> 0; matrix products, arithmetic and copies ran while one was open for 0% -> 0% of each run, Pallas kernels for 0% -> 0%
where the time goes in v1:
time: 66.6 us; the launch traced here: 66.4 us
  Pallas kernels  62.8 us (94%)
  local copies, waits for them, and re-layouts  2.91 us (4%)
  between operations  0.68 us (1%)
    pallas_call x1, Pallas kernels, reduce_call(): pl.pallas_call(reduce_kernel, out_shape=(jax.ShapeDtypeStruct((CHIPS, 8,...  54.3 us
    pallas_call x1, Pallas kernels, factor_call(): pl.pallas_call(factor_kernel, out_shape=(jax.ShapeDtypeStruct((4, RANK),...  8.55 us
    unnamed x5, local copies, waits for them, and re-layouts  2.08 us

profile of v1, /device:TPU:1, one launch (start us, length us, event | category | flops | bytes accessed | tf_op | source)
XLA Modules:
  0.0 66.4 jit_solution(8188566757015430908)
XLA Ops:
  0.6 0.0 copy-start
  0.6 1.1 %copy.6.q_hbm = f32[896,32]{1,0:T(8,128)S(1)} copy(f32[896,32]{0,1:T(8,128)} %param.5) | data formatting | bytes 229376 | tf_op args[2]
  1.8 0.0 copy-done
  1.8 0.0 copy-start.1
  1.8 0.9 %copy-done.1 = bf16[1,128,896]{2,1,0:T(8,128)(2,1)S(1)} copy-done((bf16[1,128,896]{2,1,0:T(8,128)(2,1)S(1)}, bf16[1,128,896]{2,1,0:T(8,128)(2,1)}, u32[]{:S(2)}) %copy-start.1) | copy-done | bytes 229400
  2.7 54.3 %plane_and_line_sums.1 = (f32[16,8,128]{2,1,0:T(8,128)S(1)}, f32[896,128]{1,0:T(8,128)S(1)}) custom-call(f32[1,128,896]{2,1,0:T(8,128)S(1)} %copy-done, bf16[1,128,896]{2,1,0:T(8,128)(2,1)S(1)} %copy-done.1, f32[896,32]{1,0:T(8,128)S(1)} %copy.6.q_hbm), custom_call_target="tpu_custom_call" | custom-call | tf_op jit(solution)/shard_map/plane_and_line_sums/pallas_call | solution.py:223
  57.0 8.5 %factors.1 = (f32[4,32]{1,0:T(4,128)}, f32[896,32]{1,0:T(8,128)S(1)}, bf16[1,128,896]{2,1,0:T(8,128)(2,1)}) custom-call(f32[16,8,128]{2,1,0:T(8,128)S(1)} %get-tuple-element.5.m_ref, f32[896,128]{1,0:T(8,128)S(1)} %get-tuple-element.6.st_ref, f32[1,128,896]{2,1,0:T(8,128)S(1)} %copy-done, bf16[1,128,896]{2,1,0:T(8,128)(2,1)S(1)} %copy-done.1), custom_call_target="tpu_custom_call" | custom-call | tf_op jit(solution)/shard_map/factors/pallas_call | solution.py:302
  65.6 0.8 %copy.7 = f32[896,32]{0,1:T(8,128)} copy(f32[896,32]{1,0:T(8,128)S(1)} %get-tuple-element.8) | data formatting | bytes 229376 | tf_op jit(solution)/shard_map/factors/pallas_call | solution.py:302
Async XLA Ops:
  0.6 1.2 %copy-start = (f32[1,128,896]{2,1,0:T(8,128)S(1)}, f32[1,128,896]{2,1,0:T(8,128)}, u32[]{:S(2)}) copy-start(f32[1,128,896]{2,1,0:T(8,128)} %g_hbm.3) | copy-start | bytes 1376260
  1.8 0.9 %copy-start.1 = (bf16[1,128,896]{2,1,0:T(8,128)(2,1)S(1)}, bf16[1,128,896]{2,1,0:T(8,128)(2,1)}, u32[]{:S(2)}) copy-start(bf16[1,128,896]{2,1,0:T(8,128)(2,1)} %e_hbm.3) | copy-start | bytes 688132

commit v2 on v1

--- a/solution.py
+++ b/solution.py
@@ -17,6 +17,9 @@
 SOURCES = 2 * OWNERS
 DEPTH = 32
 PLANE = 32
+REPLICAS = 32
+BLOCK = 16
+VMEM_LIMIT = (64 << 20) - (1100 << 10)
 
 
 def dot(left, right, left_dim, right_dim):
@@ -34,8 +37,8 @@
 
 
 def reduce_kernel(
-    g_hbm, e_hbm, q_hbm, m_out, st_out,
-    g_v, e_v, q_v, ct, sib, rs, part, tiles, zb,
+    g_hbm, e_hbm, qt_hbm, m_out, st_out, c_out,
+    g_v, e_v, qt_v, q_v, ct, sib, rs, part, tiles, zb,
     load_sem, sib_sem, rs_sem, tile_sem, z_sem, m_sem, st_sem, go_sem,
 ):
     dp = lax.axis_index("dp")
@@ -46,7 +49,7 @@
     loads = [
         pltpu.make_async_copy(g_hbm.at[0], g_v, load_sem.at[0]),
         pltpu.make_async_copy(e_hbm.at[0], e_v, load_sem.at[1]),
-        pltpu.make_async_copy(q_hbm, q_v, load_sem.at[2]),
+        pltpu.make_async_copy(qt_hbm, qt_v, load_sem.at[2]),
     ]
     for load in loads:
         load.start()
@@ -71,7 +74,10 @@
         load.wait()
     for b in range(COLS // 128):
         cols = slice(128 * b, 128 * b + 128)
-        ct[cols, :] = (g_v[:, cols] + e_v[:, cols].astype(jnp.float32)).T
+        corrected = g_v[:, cols] + e_v[:, cols].astype(jnp.float32)
+        c_out[:, cols] = corrected
+        ct[cols, :] = corrected.T
+        q_v[cols, :] = qt_v[:, cols].T
 
     @pl.when(core == 0)
     def _():
@@ -171,6 +177,14 @@
                 device_id=(lax.rem(dp + k, PLANE), z), device_id_type=MESH,
             ).start()
 
+    @pl.when(chip < OWNERS)
+    def _():
+        wait_bytes(st_out.at[pl.ds(0, COLS - SLICE)], st_sem.at[1])
+
+    @pl.when(chip >= OWNERS)
+    def _():
+        wait_bytes(st_out, st_sem.at[1])
+
     @pl.when(core == 1)
     def _():
         wait_bytes(zb.at[pl.ds(0, DEPTH - 1)], z_sem.at[1])
@@ -197,7 +211,6 @@
 
     @pl.when(chip < OWNERS)
     def _():
-        wait_bytes(st_out.at[pl.ds(0, COLS - SLICE)], st_sem.at[1])
         wait_bytes(ct.at[pl.ds(0, SLICE * (OWNERS - 1))], rs_sem.at[0])
         wait_bytes(st_out, st_sem.at[0])
         wait_bytes(st_out.at[pl.ds(0, COLS // 28 * 3)], st_sem.at[0])
@@ -212,25 +225,26 @@
 
     @pl.when(chip >= OWNERS)
     def _():
-        wait_bytes(st_out, st_sem.at[1])
         wait_bytes(ct.at[pl.ds(0, HALF)], rs_sem.at[0])
 
 
-def reduce_call(gradients, error_memory, q_start):
-    any_space = pl.BlockSpec(memory_space=pl.ANY)
+def reduce_call(gradients, error_memory, qt_start):
+    hbm = pl.BlockSpec(memory_space=pltpu.HBM)
     vmem = pl.BlockSpec(memory_space=pltpu.VMEM)
     pair = pltpu.SemaphoreType.DMA((2,))
     return pl.pallas_call(
         reduce_kernel,
         out_shape=(
-            jax.ShapeDtypeStruct((CHIPS, 8, 128), jnp.float32),
-            jax.ShapeDtypeStruct((COLS, ROWS), jnp.float32),
+            pltpu.VMEM((CHIPS, 8, 128), jnp.float32),
+            pltpu.VMEM((COLS, ROWS), jnp.float32),
+            pltpu.VMEM((ROWS, COLS), jnp.float32),
         ),
-        in_specs=[any_space] * 3,
-        out_specs=(vmem, vmem),
+        in_specs=[hbm] * 3,
+        out_specs=(vmem, vmem, vmem),
         scratch_shapes=[
             pltpu.VMEM((ROWS, COLS), jnp.float32),
             pltpu.VMEM((ROWS, COLS), jnp.bfloat16),
+            pltpu.VMEM((RANK, COLS), jnp.float32),
             pltpu.VMEM((COLS, RANK), jnp.float32),
             pltpu.VMEM((COLS, ROWS), jnp.float32),
             pltpu.VMEM((HALF, ROWS), jnp.float32),
@@ -243,31 +257,49 @@
             pltpu.SemaphoreType.REGULAR,
         ],
         compiler_params=pltpu.CompilerParams(
-            collective_id=0, has_side_effects=True, vmem_limit_bytes=16 << 20
+            collective_id=0, has_side_effects=True, vmem_limit_bytes=VMEM_LIMIT
         ),
         name="plane_and_line_sums",
-    )(gradients, error_memory, q_start)
+    )(gradients, error_memory, qt_start)
 
 
 def orthonormal_rows(pt):
     gram = dot(pt, pt, 1, 1)
-    row = lax.broadcasted_iota(jnp.int32, (RANK, 1), 0)
-    for k in range(RANK):
-        pivot = gram[k : k + 1, k : k + 1]
-        factor = jnp.where(row > k, gram[:, k : k + 1] / pivot, 0.0)
-        gram, pt = gram - factor * gram[k : k + 1, :], pt - factor * pt[k : k + 1, :]
-    diag = lax.broadcasted_iota(jnp.int32, (RANK, RANK), 0) == lax.broadcasted_iota(jnp.int32, (RANK, RANK), 1)
-    pivots = jnp.sum(jnp.where(diag, gram, 0.0), axis=1, keepdims=True)
-    return pt / jnp.sqrt(pivots)
-
-
-def factor_kernel(m_ref, st_ref, g_hbm, e_hbm, p_out, q_out, new_out, g_v, e_v, load_sem):
-    loads = [
-        pltpu.make_async_copy(g_hbm.at[0], g_v, load_sem.at[0]),
-        pltpu.make_async_copy(e_hbm.at[0], e_v, load_sem.at[1]),
-    ]
-    for load in loads:
-        load.start()
+    high = RANK // 8
+    gram = [gram[8 * t : 8 * t + 8] for t in range(high)]
+    rows = [pt[8 * t : 8 * t + 8] for t in range(high)]
+    pivots = [jnp.ones((8, ROWS), jnp.float32) for t in range(high)]
+    sub = lax.broadcasted_iota(jnp.int32, (8, ROWS), 0)
+    for first in range(0, RANK, BLOCK):
+        more = first + BLOCK < RANK
+        cols = [
+            [jnp.broadcast_to(gram[t][:, first + j : first + j + 1], (8, ROWS)) for t in range(high)]
+            for j in range(BLOCK)
+        ]
+        for j in range(BLOCK):
+            at, s = divmod(first + j, 8)
+            pivot = jnp.broadcast_to(cols[j][at][s : s + 1], (8, ROWS))
+            inverse = 1.0 / pivot
+            factor = [None] * high
+            for t in range(at, high):
+                factor[t] = cols[j][t] * inverse
+            factor[at] = jnp.where(sub > s, factor[at], 0.0)
+            for later in range(j + 1, BLOCK):
+                entry = jnp.broadcast_to(cols[later][at][s : s + 1], (8, ROWS))
+                for t in range(at, high):
+                    cols[later][t] = cols[later][t] - factor[t] * entry
+            row = jnp.broadcast_to(rows[at][s : s + 1], (8, ROWS))
+            for t in range(at, high):
+                rows[t] = rows[t] - factor[t] * row
+            if more:
+                line = jnp.broadcast_to(gram[at][s : s + 1], (8, RANK))
+                for t in range(at, high):
+                    gram[t] = gram[t] - factor[t][:, :RANK] * line
+            pivots[at] = jnp.where(sub == s, pivot, pivots[at])
+    return jnp.concatenate([rows[t] / jnp.sqrt(pivots[t]) for t in range(high)], axis=0)
+
+
+def factor_kernel(m_ref, st_ref, c_ref, p_out, qt_out, new_hbm, new_v, store_sem):
     pt = jnp.concatenate([m_ref[t] for t in range(4)], axis=0)
     top = jnp.concatenate([m_ref[4 + t] for t in range(8)], axis=0)
     packed = jnp.concatenate([m_ref[12 + t] for t in range(4)], axis=0)
@@ -284,43 +316,44 @@
     z = lax.axis_index("tensor")
     pick = lax.broadcasted_iota(jnp.int32, (8, ROWS), 0) + 4 * z == lax.broadcasted_iota(jnp.int32, (8, ROWS), 1)
     p_out[...] = dot(pick.astype(jnp.float32), pt, 1, 1)[0:4, :]
-    st = st_ref[...]
-    q_out[...] = dot(st, pt, 1, 1) * (1.0 / REPLICAS)
-    qt = dot(pt, st, 1, 1) * (1.0 / REPLICAS)
-    product = dot(pt, qt, 0, 0)
-    for load in loads:
-        load.wait()
-    new_out[0] = (g_v[...] + e_v[...].astype(jnp.float32) - product).astype(jnp.bfloat16)
-
-
-REPLICAS = 32
-
-
-def factor_call(tiles, st, gradients, error_memory):
-    any_space = pl.BlockSpec(memory_space=pl.ANY)
+    scaled = pt * (1.0 / REPLICAS)
+    copies = []
+    for b in range(COLS // 128):
+        cols = slice(128 * b, 128 * b + 128)
+        q = dot(st_ref[cols, :], scaled, 1, 1)
+        qt_out[:, cols] = q.T
+        new_v[:, cols] = (c_ref[:, cols] - dot(q, pt, 1, 0).T).astype(jnp.bfloat16)
+        copies.append(pltpu.make_async_copy(new_v.at[:, cols], new_hbm.at[0, :, cols], store_sem.at[b]))
+        copies[b].start()
+    for copy in copies:
+        copy.wait()
+
+
+def factor_call(tiles, st, corrected):
+    hbm = pl.BlockSpec(memory_space=pltpu.HBM)
     vmem = pl.BlockSpec(memory_space=pltpu.VMEM)
     return pl.pallas_call(
         factor_kernel,
         out_shape=(
             jax.ShapeDtypeStruct((4, RANK), jnp.float32),
-            jax.ShapeDtypeStruct((COLS, RANK), jnp.float32),
+            jax.ShapeDtypeStruct((RANK, COLS), jnp.float32),
             jax.ShapeDtypeStruct((1, ROWS, COLS), jnp.bfloat16),
         ),
-        in_specs=[vmem, vmem, any_space, any_space],
-        out_specs=(vmem, vmem, vmem),
+        in_specs=[vmem, vmem, vmem],
+        out_specs=(vmem, vmem, hbm),
         scratch_shapes=[
-            pltpu.VMEM((ROWS, COLS), jnp.float32),
             pltpu.VMEM((ROWS, COLS), jnp.bfloat16),
-            pltpu.SemaphoreType.DMA((2,)),
+            pltpu.SemaphoreType.DMA((COLS // 128,)),
         ],
-        compiler_params=pltpu.CompilerParams(vmem_limit_bytes=16 << 20),
+        compiler_params=pltpu.CompilerParams(vmem_limit_bytes=32 << 20),
         name="factors",
-    )(tiles, st, gradients, error_memory)
+    )(tiles, st, corrected)
 
 
 def local(gradients, error_memory, q_start):
-    tiles, st = reduce_call(gradients, error_memory, q_start)
-    return factor_call(tiles, st, gradients, error_memory)
+    tiles, st, corrected = reduce_call(gradients, error_memory, q_start.T)
+    p_rows, qt, new_error = factor_call(tiles, st, corrected)
+    return p_rows, qt.T, new_error
 
 
 def solution(mesh):

time: 66.6 us -> 58.6 us (0.88)
  Pallas kernels: 62.8 us -> 57.8 us
  local copies, waits for them, and re-layouts: 2.91 us -> 0 us
    pallas_call x1, Pallas kernels: 8.55 us -> 4.38 us  [factor_call(): pl.pallas_call(factor_kernel, out_shape=(jax.ShapeDtypeStruct((4, RANK),...]
    unnamed x5 -> x0, local copies, waits for them, and re-layouts: 2.08 us -> none
    pallas_call x1, Pallas kernels: 54.3 us -> 53.4 us  [reduce_call(): pl.pallas_call(reduce_kernel, out_shape=(pltpu.VMEM((CHIPS, 8, 128), jnp....]
    pallas_call x1 -> x0, local copies, waits for them, and re-layouts: 0.82 us -> none  [factor_call(): pl.pallas_call(factor_kernel, out_shape=(jax.ShapeDtypeStruct((4, RANK),...]
where the time goes in v2:
time: 58.6 us; the launch traced here: 58.5 us
  Pallas kernels  57.8 us (99%)
  between operations  0.64 us (1%)
    pallas_call x1, Pallas kernels, reduce_call(): pl.pallas_call(reduce_kernel, out_shape=(pltpu.VMEM((CHIPS, 8, 128), jnp....  53.4 us
    pallas_call x1, Pallas kernels, factor_call(): pl.pallas_call(factor_kernel, out_shape=(jax.ShapeDtypeStruct((4, RANK),...  4.38 us

profile of v2, /device:TPU:1, one launch (start us, length us, event | category | flops | bytes accessed | tf_op | source)
XLA Modules:
  0.0 58.5 jit_solution(9130130782751750855)
XLA Ops:
  0.6 53.4 %plane_and_line_sums.1 = (f32[16,8,128]{2,1,0:T(8,128)S(1)}, f32[896,128]{1,0:T(8,128)S(1)}, f32[128,896]{1,0:T(8,128)S(1)}) custom-call(f32[1,128,896]{2,1,0:T(8,128)} %g_hbm.1, bf16[1,128,896]{2,1,0:T(8,128)(2,1)} %e_hbm.1, f32[32,896]{1,0:T(8,128)} %bitcast.2), custom_call_target="tpu_custom_call" | custom-call | tf_op jit(solution)/shard_map/plane_and_line_sums/pallas_call | solution.py:235
  54.1 4.4 %factors.1 = (f32[4,32]{1,0:T(4,128)}, f32[32,896]{1,0:T(8,128)}, bf16[1,128,896]{2,1,0:T(8,128)(2,1)}) custom-call(f32[16,8,128]{2,1,0:T(8,128)S(1)} %get-tuple-element.9.m_ref, f32[896,128]{1,0:T(8,128)S(1)} %get-tuple-element.10.st_ref, f32[128,896]{1,0:T(8,128)S(1)} %get-tuple-element.11.c_ref), custom_call_target="tpu_custom_call" | custom-call | tf_op jit(solution)/shard_map/factors/pallas_call | solution.py:335

commit v3 on v2

--- a/solution.py
+++ b/solution.py
@@ -6,6 +6,11 @@
 from jax.sharding import PartitionSpec as P
 
 MESH = pl.DeviceIdType.MESH
+SIDE = 4
+OFFSETS = sorted(
+    ((dx, dy) for dx in range(SIDE) for dy in range(SIDE) if dx or dy),
+    key=lambda d: -(min(d[0], SIDE - d[0]) + min(d[1], SIDE - d[1])),
+)
 HIGH = lax.Precision.HIGHEST
 ROWS = 128
 COLS = 896
@@ -19,6 +24,7 @@
 PLANE = 32
 REPLICAS = 32
 BLOCK = 16
+STEPS = (0, 256, 512, 896)
 VMEM_LIMIT = (64 << 20) - (1100 << 10)
 
 
@@ -32,14 +38,24 @@
     )
 
 
+def halves(value):
+    high = value.astype(jnp.bfloat16)
+    return high, (value - high.astype(jnp.float32)).astype(jnp.bfloat16)
+
+
 def wait_bytes(ref, sem):
     pltpu.make_async_copy(ref, ref, sem).wait()
 
 
+def shifted(chip, offset):
+    x, y = lax.div(chip, SIDE), lax.rem(chip, SIDE)
+    return SIDE * lax.rem(x + offset[0], SIDE) + lax.rem(y + offset[1], SIDE)
+
+
 def reduce_kernel(
-    g_hbm, e_hbm, qt_hbm, m_out, st_out, c_out,
-    g_v, e_v, qt_v, q_v, ct, sib, rs, part, tiles, zb,
-    load_sem, sib_sem, rs_sem, tile_sem, z_sem, m_sem, st_sem, go_sem,
+    g_hbm, e_hbm, qt_hbm, m_out, s_out, c_out,
+    g_v, e_v, qt_v, q_v, ct, sib, rs, part, tiles, zb, st_v,
+    load_sem, sib_sem, rs_sem, tile_sem, z_sem, m_sem, st_sem, go_sem, later_sem,
 ):
     dp = lax.axis_index("dp")
     z = lax.axis_index("tensor")
@@ -98,9 +114,10 @@
     swap.wait_recv()
     ct[pl.ds(mine, HALF), :] += sib[...]
 
-    @pl.loop(0, OWNERS)
-    def _(j):
-        @pl.when(j != chip)
+    for offset in OFFSETS:
+        j = shifted(chip, offset)
+
+        @pl.when(j < OWNERS)
         def _():
             pltpu.make_async_remote_copy(
                 src_ref=ct.at[pl.ds(pl.multiple_of(mine + SLICE * j, 8), SLICE)], dst_ref=rs.at[chip],
@@ -118,7 +135,7 @@
         total = rs[0]
         for j in range(1, CHIPS):
             total += rs[j]
-        st_out[pl.ds(own, SLICE), :] = total
+        st_v[pl.ds(own, SLICE), :] = total
         gram = dot(total, total, 0, 0)
         left = dot(q_v[pl.ds(own, SLICE), :], total, 0, 0)
         for t in range(4):
@@ -132,14 +149,18 @@
         for t in range(4):
             part[12 + t] = packed[8 * t : 8 * t + 8]
 
-        @pl.loop(0, CHIPS)
-        def _(j):
-            @pl.when(2 * j + 1 != dp)
-            def _():
-                pltpu.make_async_remote_copy(
-                    src_ref=part.at[j], dst_ref=tiles.at[source], send_sem=tile_sem.at[0], recv_sem=tile_sem.at[1],
-                    device_id=(2 * j + 1, z), device_id_type=MESH,
-                ).start()
+        def send_tile(j):
+            pltpu.make_async_remote_copy(
+                src_ref=part.at[j], dst_ref=tiles.at[source], send_sem=tile_sem.at[0], recv_sem=tile_sem.at[1],
+                device_id=(2 * j + 1, z), device_id_type=MESH,
+            ).start()
+
+        for offset in OFFSETS:
+            send_tile(shifted(chip, offset))
+
+        @pl.when(core == 0)
+        def _():
+            send_tile(chip)
 
     @pl.when(core == 1)
     def _():
@@ -167,23 +188,35 @@
                 device_id=(dp, lax.rem(z + shift, DEPTH)), device_id_type=MESH,
             ).start()
 
+        pl.semaphore_signal(later_sem, inc=1, device_id=(dp - 1, z), device_id_type=MESH)
+
+    @pl.when(core == 0)
+    def _():
+        pl.semaphore_wait(later_sem, 1)
+
     @pl.when(chip < OWNERS)
     def _():
         @pl.loop(1, PLANE)
         def _(k):
             pltpu.make_async_remote_copy(
-                src_ref=st_out.at[pl.ds(own, SLICE)], dst_ref=st_out.at[pl.ds(own, SLICE)],
+                src_ref=st_v.at[pl.ds(own, SLICE)], dst_ref=st_v.at[pl.ds(own, SLICE)],
                 send_sem=st_sem.at[0], recv_sem=st_sem.at[1],
                 device_id=(lax.rem(dp + k, PLANE), z), device_id_type=MESH,
             ).start()
 
     @pl.when(chip < OWNERS)
     def _():
-        wait_bytes(st_out.at[pl.ds(0, COLS - SLICE)], st_sem.at[1])
+        wait_bytes(st_v.at[pl.ds(0, COLS - SLICE)], st_sem.at[1])
 
     @pl.when(chip >= OWNERS)
     def _():
-        wait_bytes(st_out, st_sem.at[1])
+        wait_bytes(st_v, st_sem.at[1])
+
+    for b in range(COLS // 128):
+        cols = slice(128 * b, 128 * b + 128)
+        high, low = halves(st_v[cols, :].T)
+        s_out[0:ROWS, cols] = high
+        s_out[ROWS : 2 * ROWS, cols] = low
 
     @pl.when(core == 1)
     def _():
@@ -193,12 +226,17 @@
             total += zb[j]
         m_out[chip] = total
 
-        @pl.loop(1, PLANE)
-        def _(k):
+        def send_sum(device):
             pltpu.make_async_remote_copy(
                 src_ref=m_out.at[chip], dst_ref=m_out.at[chip], send_sem=m_sem.at[0], recv_sem=m_sem.at[1],
-                device_id=(lax.rem(dp + k, PLANE), z), device_id_type=MESH,
+                device_id=(device, z), device_id_type=MESH,
             ).start()
+
+        for offset in OFFSETS:
+            j = shifted(chip, offset)
+            send_sum(2 * j)
+            send_sum(2 * j + 1)
+        send_sum(dp - 1)
         wait_bytes(m_out.at[pl.ds(0, CHIPS - 1)], m_sem.at[1])
         wait_bytes(zb.at[pl.ds(0, DEPTH - 1)], z_sem.at[0])
         wait_bytes(zb.at[pl.ds(0, PLANE - 1)], m_sem.at[0])
@@ -212,8 +250,8 @@
     @pl.when(chip < OWNERS)
     def _():
         wait_bytes(ct.at[pl.ds(0, SLICE * (OWNERS - 1))], rs_sem.at[0])
-        wait_bytes(st_out, st_sem.at[0])
-        wait_bytes(st_out.at[pl.ds(0, COLS // 28 * 3)], st_sem.at[0])
+        wait_bytes(st_v, st_sem.at[0])
+        wait_bytes(st_v.at[pl.ds(0, COLS // 28 * 3)], st_sem.at[0])
 
         @pl.when(core == 0)
         def _():
@@ -236,7 +274,7 @@
         reduce_kernel,
         out_shape=(
             pltpu.VMEM((CHIPS, 8, 128), jnp.float32),
-            pltpu.VMEM((COLS, ROWS), jnp.float32),
+            pltpu.VMEM((2 * ROWS, COLS), jnp.bfloat16),
             pltpu.VMEM((ROWS, COLS), jnp.float32),
         ),
         in_specs=[hbm] * 3,
@@ -252,8 +290,10 @@
             pltpu.VMEM((CHIPS, 8, 128), jnp.float32),
             pltpu.VMEM((SOURCES, 8, 128), jnp.float32),
             pltpu.VMEM((DEPTH, 8, 128), jnp.float32),
+            pltpu.VMEM((COLS, ROWS), jnp.float32),
             pltpu.SemaphoreType.DMA((3,)),
             pair, pair, pair, pair, pair, pair,
+            pltpu.SemaphoreType.REGULAR,
             pltpu.SemaphoreType.REGULAR,
         ],
         compiler_params=pltpu.CompilerParams(
@@ -299,7 +339,7 @@
     return jnp.concatenate([rows[t] / jnp.sqrt(pivots[t]) for t in range(high)], axis=0)
 
 
-def factor_kernel(m_ref, st_ref, c_ref, p_out, qt_out, new_hbm, new_v, store_sem):
+def factor_kernel(m_ref, s_ref, c_ref, p_hbm, qt_hbm, new_hbm, p_v, qt_v, new_v, store_sem):
     pt = jnp.concatenate([m_ref[t] for t in range(4)], axis=0)
     top = jnp.concatenate([m_ref[4 + t] for t in range(8)], axis=0)
     packed = jnp.concatenate([m_ref[12 + t] for t in range(4)], axis=0)
@@ -313,23 +353,40 @@
     second = dot(first, gram, 1, 0) * (1.0 / REPLICAS)
     pt = orthonormal_rows(second)
 
+    left = pt.T
     z = lax.axis_index("tensor")
-    pick = lax.broadcasted_iota(jnp.int32, (8, ROWS), 0) + 4 * z == lax.broadcasted_iota(jnp.int32, (8, ROWS), 1)
-    p_out[...] = dot(pick.astype(jnp.float32), pt, 1, 1)[0:4, :]
-    scaled = pt * (1.0 / REPLICAS)
-    copies = []
-    for b in range(COLS // 128):
-        cols = slice(128 * b, 128 * b + 128)
-        q = dot(st_ref[cols, :], scaled, 1, 1)
-        qt_out[:, cols] = q.T
-        new_v[:, cols] = (c_ref[:, cols] - dot(q, pt, 1, 0).T).astype(jnp.bfloat16)
-        copies.append(pltpu.make_async_copy(new_v.at[:, cols], new_hbm.at[0, :, cols], store_sem.at[b]))
-        copies[b].start()
+    p_v[0:ROWS, :] = left
+    pair = p_v[pl.ds(pl.multiple_of(8 * lax.div(z, 2), 8), 8), :]
+    p_v[ROWS : ROWS + 4, :] = jnp.where(lax.rem(z, 2) == 0, pair[0:4], pair[4:8])
+    copies = [pltpu.make_async_copy(p_v.at[pl.ds(ROWS, 4)], p_hbm, store_sem.at[0])]
+    copies[0].start()
+
+    high, low = halves(pt)
+    zero = jnp.zeros_like(low)
+    rows = jnp.concatenate(
+        [jnp.concatenate([high, high], axis=1), jnp.concatenate([low, zero], axis=1)], axis=0
+    )
+    high, low = halves(left)
+    thrice = jnp.concatenate([high, high, low], axis=1)
+    for b in range(len(STEPS) - 1):
+        cols = slice(STEPS[b], STEPS[b + 1])
+        both = jnp.dot(rows, s_ref[:, cols], preferred_element_type=jnp.float32)
+        qt = (both[0:RANK] + both[RANK : 2 * RANK]) * (1.0 / REPLICAS)
+        qt_v[:, cols] = qt
+        high, low = halves(qt)
+        product = jnp.dot(
+            thrice, jnp.concatenate([high, low, high], axis=0), preferred_element_type=jnp.float32
+        )
+        new_v[:, cols] = (c_ref[:, cols] - product).astype(jnp.bfloat16)
+        copies.append(pltpu.make_async_copy(new_v.at[:, cols], new_hbm.at[0, :, cols], store_sem.at[b + 2]))
+        copies[-1].start()
+    copies.append(pltpu.make_async_copy(qt_v, qt_hbm, store_sem.at[1]))
+    copies[-1].start()
     for copy in copies:
         copy.wait()
 
 
-def factor_call(tiles, st, corrected):
+def factor_call(tiles, split, corrected):
     hbm = pl.BlockSpec(memory_space=pltpu.HBM)
     vmem = pl.BlockSpec(memory_space=pltpu.VMEM)
     return pl.pallas_call(
@@ -340,19 +397,21 @@
             jax.ShapeDtypeStruct((1, ROWS, COLS), jnp.bfloat16),
         ),
         in_specs=[vmem, vmem, vmem],
-        out_specs=(vmem, vmem, hbm),
+        out_specs=(hbm, hbm, hbm),
         scratch_shapes=[
+            pltpu.VMEM((ROWS + 8, RANK), jnp.float32),
+            pltpu.VMEM((RANK, COLS), jnp.float32),
             pltpu.VMEM((ROWS, COLS), jnp.bfloat16),
-            pltpu.SemaphoreType.DMA((COLS // 128,)),
+            pltpu.SemaphoreType.DMA((len(STEPS) + 1,)),
         ],
         compiler_params=pltpu.CompilerParams(vmem_limit_bytes=32 << 20),
         name="factors",
-    )(tiles, st, corrected)
+    )(tiles, split, corrected)
 
 
 def local(gradients, error_memory, q_start):
-    tiles, st, corrected = reduce_call(gradients, error_memory, q_start.T)
-    p_rows, qt, new_error = factor_call(tiles, st, corrected)
+    tiles, split, corrected = reduce_call(gradients, error_memory, q_start.T)
+    p_rows, qt, new_error = factor_call(tiles, split, corrected)
     return p_rows, qt.T, new_error
 
 

time: 58.6 us -> 55.4 us (0.945)
  Pallas kernels: 57.8 us -> 54.6 us
    pallas_call x1, Pallas kernels: 53.4 us -> 51.5 us  [reduce_call(): pl.pallas_call(reduce_kernel, out_shape=(pltpu.VMEM((CHIPS, 8, 128), jnp....]
    pallas_call x1, Pallas kernels: 4.38 us -> 3.13 us  [factor_call(): pl.pallas_call(factor_kernel, out_shape=(jax.ShapeDtypeStruct((4, RANK),...]
where the time goes in v3:
time: 55.4 us; the launch traced here: 55.3 us
  Pallas kernels  54.6 us (99%)
  between operations  0.64 us (1%)
    pallas_call x1, Pallas kernels, reduce_call(): pl.pallas_call(reduce_kernel, out_shape=(pltpu.VMEM((CHIPS, 8, 128), jnp....  51.5 us
    pallas_call x1, Pallas kernels, factor_call(): pl.pallas_call(factor_kernel, out_shape=(jax.ShapeDtypeStruct((4, RANK),...  3.13 us

profile of v3, /device:TPU:1, one launch (start us, length us, event | category | flops | bytes accessed | tf_op | source)
XLA Modules:
  0.0 55.3 jit_solution(9974675196469401694)
XLA Ops:
  0.6 51.5 %plane_and_line_sums.1 = (f32[16,8,128]{2,1,0:T(8,128)S(1)}, bf16[256,896]{1,0:T(8,128)(2,1)S(1)}, f32[128,896]{1,0:T(8,128)S(1)}) custom-call(f32[1,128,896]{2,1,0:T(8,128)} %g_hbm.1, bf16[1,128,896]{2,1,0:T(8,128)(2,1)} %e_hbm.1, f32[32,896]{1,0:T(8,128)} %bitcast.2), custom_call_target="tpu_custom_call" | custom-call | tf_op jit(solution)/shard_map/plane_and_line_sums/pallas_call | solution.py:273
  52.1 3.1 %factors.1 = (f32[4,32]{1,0:T(4,128)}, f32[32,896]{1,0:T(8,128)}, bf16[1,128,896]{2,1,0:T(8,128)(2,1)}) custom-call(f32[16,8,128]{2,1,0:T(8,128)S(1)} %get-tuple-element.9.m_ref, bf16[256,896]{1,0:T(8,128)(2,1)S(1)} %get-tuple-element.10.s_ref, f32[128,896]{1,0:T(8,128)S(1)} %get-tuple-element.11.c_ref), custom_call_target="tpu_custom_call" | custom-call | tf_op jit(solution)/shard_map/factors/pallas_call | solution.py:392

commit v4 on v3

--- a/solution.py
+++ b/solution.py
@@ -22,10 +22,12 @@
 SOURCES = 2 * OWNERS
 DEPTH = 32
 PLANE = 32
+P_TILES = 4
+P_STRIDE = 5
 REPLICAS = 32
 BLOCK = 16
 STEPS = (0, 256, 512, 896)
-VMEM_LIMIT = (64 << 20) - (1100 << 10)
+VMEM_LIMIT = (64 << 20) - (1120 << 10)
 
 
 def dot(left, right, left_dim, right_dim):
@@ -43,6 +45,16 @@
     return high, (value - high.astype(jnp.float32)).astype(jnp.bfloat16)
 
 
+def gram_of(value):
+    high = value.astype(jnp.bfloat16)
+    rest = value - high.astype(jnp.float32)
+    middle = rest.astype(jnp.bfloat16)
+    low = (rest - middle.astype(jnp.float32)).astype(jnp.bfloat16)
+    left = jnp.concatenate([high, high, high, middle, middle, low], axis=0)
+    right = jnp.concatenate([high, middle, low, high, middle, high], axis=0)
+    return lax.dot_general(left, right, (((0,), (0,)), ((), ())), preferred_element_type=jnp.float32)
+
+
 def wait_bytes(ref, sem):
     pltpu.make_async_copy(ref, ref, sem).wait()
 
@@ -53,14 +65,36 @@
 
 
 def reduce_kernel(
-    g_hbm, e_hbm, qt_hbm, m_out, s_out, c_out,
-    g_v, e_v, qt_v, q_v, ct, sib, rs, part, tiles, zb, st_v,
-    load_sem, sib_sem, rs_sem, tile_sem, z_sem, m_sem, st_sem, go_sem, later_sem,
+    g_hbm, e_hbm, qt_hbm, m_out, s_out, c_out, first_out,
+    g_v, e_v, qt_v, ct, sib, rs, part, tiles, zb, st_v, p_part, p_tiles, p_zb, p_v,
+    load_sem, swap_sem, rs_sem, tile_sem, z_sem, m_sem, st_sem, pt_sem, pz_sem, p_sem, go_sem, later_sem,
 ):
     dp = lax.axis_index("dp")
     z = lax.axis_index("tensor")
     core = lax.rem(dp, 2)
     chip = lax.div(dp, 2)
+    holds_p = jnp.logical_and(core == 1, lax.rem(chip, P_STRIDE) == 0)
+    p_mine = lax.div(chip, P_STRIDE)
+
+    def send(src, dst, sems, device):
+        pltpu.make_async_remote_copy(
+            src_ref=src, dst_ref=dst, send_sem=sems.at[0], recv_sem=sems.at[1],
+            device_id=device, device_id_type=MESH,
+        ).start()
+
+    def send_line(buffer, sems):
+        @pl.loop(0, DEPTH - 1)
+        def _(k):
+            half = lax.div(k + 1, 2)
+            shift = jnp.where(lax.rem(k, 2) == 0, DEPTH // 2 + half, DEPTH // 2 - half)
+            send(buffer.at[z], buffer.at[z], sems, (dp, lax.rem(z + shift, DEPTH)))
+
+    def send_plane(ref, sems):
+        for offset in OFFSETS:
+            j = shifted(chip, offset)
+            send(ref, ref, sems, (2 * j, z))
+            send(ref, ref, sems, (2 * j + 1, z))
+        send(ref, ref, sems, (dp - 1, z))
 
     loads = [
         pltpu.make_async_copy(g_hbm.at[0], g_v, load_sem.at[0]),
@@ -72,14 +106,13 @@
 
     barrier = pltpu.get_barrier_semaphore()
 
-    @pl.loop(0, CHIPS)
-    def _(j):
-        @pl.when(2 * j != dp)
-        def _():
-            pl.semaphore_signal(barrier, inc=1, device_id=(2 * j, z), device_id_type=MESH)
+    for offset in OFFSETS:
+        pl.semaphore_signal(barrier, inc=1, device_id=(2 * shifted(chip, offset), z), device_id_type=MESH)
 
     @pl.when(core == 1)
     def _():
+        pl.semaphore_signal(barrier, inc=1, device_id=(dp - 1, z), device_id_type=MESH)
+
         @pl.loop(1, DEPTH)
         def _(k):
             pl.semaphore_signal(
@@ -93,7 +126,9 @@
         corrected = g_v[:, cols] + e_v[:, cols].astype(jnp.float32)
         c_out[:, cols] = corrected
         ct[cols, :] = corrected.T
-        q_v[cols, :] = qt_v[:, cols].T
+
+    def left_terms():
+        p_part[...] = dot(qt_v[...], ct[...], 1, 0).reshape(P_TILES, 8, ROWS)
 
     @pl.when(core == 0)
     def _():
@@ -102,68 +137,76 @@
 
     @pl.when(core == 1)
     def _():
+        left_terms()
         pl.semaphore_wait(go_sem, 1)
 
-    mine = pl.multiple_of(core * HALF, 8)
-    other = pl.multiple_of((1 - core) * HALF, 8)
+    mine = core * HALF
+    other = (1 - core) * HALF
+    sibling = dp + 1 - 2 * core
+
     swap = pltpu.make_async_remote_copy(
-        src_ref=ct.at[pl.ds(other, HALF)], dst_ref=sib, send_sem=sib_sem.at[0], recv_sem=sib_sem.at[1],
-        device_id=(dp + 1 - 2 * core, z), device_id_type=MESH,
+        src_ref=ct.at[pl.ds(pl.multiple_of(other, 8), HALF)], dst_ref=sib,
+        send_sem=swap_sem.at[0], recv_sem=swap_sem.at[1], device_id=(sibling, z), device_id_type=MESH,
     )
     swap.start()
+
+    @pl.when(core == 0)
+    def _():
+        left_terms()
+
+    for t in range(P_TILES):
+        target = 2 * P_STRIDE * t + 1
+
+        @pl.when(dp != target)
+        def _():
+            send(p_part.at[t], p_tiles.at[dp], pt_sem, (target, z))
+
     swap.wait_recv()
-    ct[pl.ds(mine, HALF), :] += sib[...]
-
+    ct[pl.ds(pl.multiple_of(mine, 8), HALF), :] += sib[...]
     for offset in OFFSETS:
         j = shifted(chip, offset)
 
         @pl.when(j < OWNERS)
         def _():
-            pltpu.make_async_remote_copy(
-                src_ref=ct.at[pl.ds(pl.multiple_of(mine + SLICE * j, 8), SLICE)], dst_ref=rs.at[chip],
-                send_sem=rs_sem.at[0], recv_sem=rs_sem.at[1],
-                device_id=(2 * j + core, z), device_id_type=MESH,
-            ).start()
-
-    own = pl.multiple_of(mine + SLICE * lax.min(chip, OWNERS - 1), 8)
-    source = core * OWNERS + lax.min(chip, OWNERS - 1)
+            piece = pl.ds(pl.multiple_of(mine + SLICE * j, 8), SLICE)
+            send(ct.at[piece], rs.at[chip], rs_sem, (2 * j + core, z))
+
+    slot = lax.min(chip, OWNERS - 1)
+    own = pl.ds(pl.multiple_of(mine + SLICE * slot, 8), SLICE)
+    source = core * OWNERS + slot
 
     @pl.when(chip < OWNERS)
     def _():
-        rs[chip] = ct[pl.ds(own, SLICE), :]
+        rs[chip] = ct[own, :]
         wait_bytes(rs.at[pl.ds(0, CHIPS - 1)], rs_sem.at[1])
         total = rs[0]
         for j in range(1, CHIPS):
             total += rs[j]
-        st_v[pl.ds(own, SLICE), :] = total
-        gram = dot(total, total, 0, 0)
-        left = dot(q_v[pl.ds(own, SLICE), :], total, 0, 0)
-        for t in range(4):
-            part[t] = left[8 * t : 8 * t + 8]
-        for t in range(8):
-            part[4 + t] = gram[8 * t : 8 * t + 8]
-        upper = gram[64:96, :]
-        lower = pltpu.roll(gram[96:128, :], 64, 1)
-        lane = lax.broadcasted_iota(jnp.int32, (32, 128), 1)
-        packed = jnp.where(lane < 64, lower, upper)
-        for t in range(4):
-            part[12 + t] = packed[8 * t : 8 * t + 8]
-
-        def send_tile(j):
-            pltpu.make_async_remote_copy(
-                src_ref=part.at[j], dst_ref=tiles.at[source], send_sem=tile_sem.at[0], recv_sem=tile_sem.at[1],
-                device_id=(2 * j + 1, z), device_id_type=MESH,
-            ).start()
+        part[...] = gram_of(total).reshape(CHIPS, 8, ROWS)
+        st_v[own, :] = total
 
         for offset in OFFSETS:
-            send_tile(shifted(chip, offset))
+            j = shifted(chip, offset)
+            send(part.at[j], tiles.at[source], tile_sem, (2 * j + 1, z))
 
         @pl.when(core == 0)
         def _():
-            send_tile(chip)
+            send(part.at[chip], tiles.at[source], tile_sem, (dp + 1, z))
 
     @pl.when(core == 1)
     def _():
+        pl.semaphore_wait(barrier, DEPTH - 1)
+
+        @pl.when(holds_p)
+        def _():
+            p_tiles[dp] = p_part[p_mine]
+            wait_bytes(p_tiles.at[pl.ds(0, PLANE - 1)], pt_sem.at[1])
+            total = p_tiles[0]
+            for j in range(1, PLANE):
+                total += p_tiles[j]
+            p_zb[z] = total
+            send_line(p_zb, pz_sem)
+
         @pl.when(chip < OWNERS)
         def _():
             tiles[source] = part[chip]
@@ -177,17 +220,7 @@
         for j in range(1, SOURCES):
             total += tiles[j]
         zb[z] = total
-        pl.semaphore_wait(barrier, DEPTH - 1)
-
-        @pl.loop(0, DEPTH - 1)
-        def _(k):
-            half = lax.div(k + 1, 2)
-            shift = jnp.where(lax.rem(k, 2) == 0, 16 + half, 16 - half)
-            pltpu.make_async_remote_copy(
-                src_ref=zb.at[z], dst_ref=zb.at[z], send_sem=z_sem.at[0], recv_sem=z_sem.at[1],
-                device_id=(dp, lax.rem(z + shift, DEPTH)), device_id_type=MESH,
-            ).start()
-
+        send_line(zb, z_sem)
         pl.semaphore_signal(later_sem, inc=1, device_id=(dp - 1, z), device_id_type=MESH)
 
     @pl.when(core == 0)
@@ -198,14 +231,8 @@
     def _():
         @pl.loop(1, PLANE)
         def _(k):
-            pltpu.make_async_remote_copy(
-                src_ref=st_v.at[pl.ds(own, SLICE)], dst_ref=st_v.at[pl.ds(own, SLICE)],
-                send_sem=st_sem.at[0], recv_sem=st_sem.at[1],
-                device_id=(lax.rem(dp + k, PLANE), z), device_id_type=MESH,
-            ).start()
-
-    @pl.when(chip < OWNERS)
-    def _():
+            send(st_v.at[own], st_v.at[own], st_sem, (lax.rem(dp + k, PLANE), z))
+
         wait_bytes(st_v.at[pl.ds(0, COLS - SLICE)], st_sem.at[1])
 
     @pl.when(chip >= OWNERS)
@@ -218,6 +245,15 @@
         s_out[0:ROWS, cols] = high
         s_out[ROWS : 2 * ROWS, cols] = low
 
+    @pl.when(holds_p)
+    def _():
+        wait_bytes(p_zb.at[pl.ds(0, DEPTH - 1)], pz_sem.at[1])
+        total = p_zb[0]
+        for j in range(1, DEPTH):
+            total += p_zb[j]
+        p_v[p_mine] = total
+        send_plane(p_v.at[p_mine], p_sem)
+
     @pl.when(core == 1)
     def _():
         wait_bytes(zb.at[pl.ds(0, DEPTH - 1)], z_sem.at[1])
@@ -225,27 +261,39 @@
         for j in range(1, DEPTH):
             total += zb[j]
         m_out[chip] = total
-
-        def send_sum(device):
-            pltpu.make_async_remote_copy(
-                src_ref=m_out.at[chip], dst_ref=m_out.at[chip], send_sem=m_sem.at[0], recv_sem=m_sem.at[1],
-                device_id=(device, z), device_id_type=MESH,
-            ).start()
-
-        for offset in OFFSETS:
-            j = shifted(chip, offset)
-            send_sum(2 * j)
-            send_sum(2 * j + 1)
-        send_sum(dp - 1)
+        send_plane(m_out.at[chip], m_sem)
+
+    @pl.when(holds_p)
+    def _():
+        wait_bytes(p_v.at[pl.ds(0, P_TILES - 1)], p_sem.at[1])
+
+    @pl.when(jnp.logical_not(holds_p))
+    def _():
+        wait_bytes(p_v, p_sem.at[1])
+
+    first_out[...] = orthonormal_rows(p_v[...].reshape(RANK, ROWS))
+
+    @pl.when(core == 0)
+    def _():
+        wait_bytes(m_out, m_sem.at[1])
+
+    @pl.when(core == 1)
+    def _():
         wait_bytes(m_out.at[pl.ds(0, CHIPS - 1)], m_sem.at[1])
         wait_bytes(zb.at[pl.ds(0, DEPTH - 1)], z_sem.at[0])
         wait_bytes(zb.at[pl.ds(0, PLANE - 1)], m_sem.at[0])
 
-    @pl.when(core == 0)
-    def _():
-        wait_bytes(m_out, m_sem.at[1])
-
     swap.wait_send()
+
+    @pl.when(holds_p)
+    def _():
+        wait_bytes(p_zb.at[pl.ds(0, DEPTH - 1)], pz_sem.at[0])
+        wait_bytes(p_zb.at[pl.ds(0, PLANE - 1)], p_sem.at[0])
+        wait_bytes(p_part.at[pl.ds(0, P_TILES - 1)], pt_sem.at[0])
+
+    @pl.when(jnp.logical_not(holds_p))
+    def _():
+        wait_bytes(p_part, pt_sem.at[0])
 
     @pl.when(chip < OWNERS)
     def _():
@@ -273,26 +321,30 @@
     return pl.pallas_call(
         reduce_kernel,
         out_shape=(
-            pltpu.VMEM((CHIPS, 8, 128), jnp.float32),
+            pltpu.VMEM((CHIPS, 8, ROWS), jnp.float32),
             pltpu.VMEM((2 * ROWS, COLS), jnp.bfloat16),
             pltpu.VMEM((ROWS, COLS), jnp.float32),
+            pltpu.VMEM((RANK, ROWS), jnp.float32),
         ),
         in_specs=[hbm] * 3,
-        out_specs=(vmem, vmem, vmem),
+        out_specs=(vmem,) * 4,
         scratch_shapes=[
             pltpu.VMEM((ROWS, COLS), jnp.float32),
             pltpu.VMEM((ROWS, COLS), jnp.bfloat16),
             pltpu.VMEM((RANK, COLS), jnp.float32),
-            pltpu.VMEM((COLS, RANK), jnp.float32),
             pltpu.VMEM((COLS, ROWS), jnp.float32),
             pltpu.VMEM((HALF, ROWS), jnp.float32),
             pltpu.VMEM((CHIPS, SLICE, ROWS), jnp.float32),
-            pltpu.VMEM((CHIPS, 8, 128), jnp.float32),
-            pltpu.VMEM((SOURCES, 8, 128), jnp.float32),
-            pltpu.VMEM((DEPTH, 8, 128), jnp.float32),
+            pltpu.VMEM((CHIPS, 8, ROWS), jnp.float32),
+            pltpu.VMEM((SOURCES, 8, ROWS), jnp.float32),
+            pltpu.VMEM((DEPTH, 8, ROWS), jnp.float32),
             pltpu.VMEM((COLS, ROWS), jnp.float32),
+            pltpu.VMEM((P_TILES, 8, ROWS), jnp.float32),
+            pltpu.VMEM((PLANE, 8, ROWS), jnp.float32),
+            pltpu.VMEM((DEPTH, 8, ROWS), jnp.float32),
+            pltpu.VMEM((P_TILES, 8, ROWS), jnp.float32),
             pltpu.SemaphoreType.DMA((3,)),
-            pair, pair, pair, pair, pair, pair,
+            pair, pair, pair, pair, pair, pair, pair, pair, pair,
             pltpu.SemaphoreType.REGULAR,
             pltpu.SemaphoreType.REGULAR,
         ],
@@ -339,20 +391,9 @@
     return jnp.concatenate([rows[t] / jnp.sqrt(pivots[t]) for t in range(high)], axis=0)
 
 
-def factor_kernel(m_ref, s_ref, c_ref, p_hbm, qt_hbm, new_hbm, p_v, qt_v, new_v, store_sem):
-    pt = jnp.concatenate([m_ref[t] for t in range(4)], axis=0)
-    top = jnp.concatenate([m_ref[4 + t] for t in range(8)], axis=0)
-    packed = jnp.concatenate([m_ref[12 + t] for t in range(4)], axis=0)
-    lane = lax.broadcasted_iota(jnp.int32, (64, 128), 1)
-    right = jnp.concatenate([packed, pltpu.roll(packed, 64, 1)], axis=0)
-    wide = jnp.concatenate([top, top], axis=0).T
-    bottom = jnp.where(lane < 64, wide[64:128, :], right)
-    gram = jnp.concatenate([top, bottom], axis=0)
-
-    first = orthonormal_rows(pt)
-    second = dot(first, gram, 1, 0) * (1.0 / REPLICAS)
+def factor_kernel(m_ref, s_ref, c_ref, first_ref, p_hbm, qt_hbm, new_hbm, p_v, qt_v, new_v, store_sem):
+    second = dot(first_ref[...], m_ref[...].reshape(ROWS, ROWS), 1, 0) * (1.0 / REPLICAS)
     pt = orthonormal_rows(second)
-
     left = pt.T
     z = lax.axis_index("tensor")
     p_v[0:ROWS, :] = left
@@ -386,7 +427,7 @@
         copy.wait()
 
 
-def factor_call(tiles, split, corrected):
+def factor_call(tiles, split, corrected, first):
     hbm = pl.BlockSpec(memory_space=pltpu.HBM)
     vmem = pl.BlockSpec(memory_space=pltpu.VMEM)
     return pl.pallas_call(
@@ -396,7 +437,7 @@
             jax.ShapeDtypeStruct((RANK, COLS), jnp.float32),
             jax.ShapeDtypeStruct((1, ROWS, COLS), jnp.bfloat16),
         ),
-        in_specs=[vmem, vmem, vmem],
+        in_specs=[vmem, vmem, vmem, vmem],
         out_specs=(hbm, hbm, hbm),
         scratch_shapes=[
             pltpu.VMEM((ROWS + 8, RANK), jnp.float32),
@@ -406,12 +447,12 @@
         ],
         compiler_params=pltpu.CompilerParams(vmem_limit_bytes=32 << 20),
         name="factors",
-    )(tiles, split, corrected)
+    )(tiles, split, corrected, first)
 
 
 def local(gradients, error_memory, q_start):
-    tiles, split, corrected = reduce_call(gradients, error_memory, q_start.T)
-    p_rows, qt, new_error = factor_call(tiles, split, corrected)
+    tiles, split, corrected, first = reduce_call(gradients, error_memory, q_start.T)
+    p_rows, qt, new_error = factor_call(tiles, split, corrected, first)
     return p_rows, qt.T, new_error
 
 

time: 55.4 us -> 54.6 us (0.986)
  Pallas kernels: 54.6 us -> 53.8 us
    pallas_call x1, Pallas kernels: 3.13 us -> 2.23 us  [factor_call(): pl.pallas_call(factor_kernel, out_shape=(jax.ShapeDtypeStruct((4, RANK),...]
where the time goes in v4:
time: 54.6 us; the launch traced here: 54.5 us
  Pallas kernels  53.8 us (99%)
  between operations  0.64 us (1%)
    pallas_call x1, Pallas kernels, reduce_call(): pl.pallas_call(reduce_kernel, out_shape=(pltpu.VMEM((CHIPS, 8, ROWS), jnp...  51.6 us
    pallas_call x1, Pallas kernels, factor_call(): pl.pallas_call(factor_kernel, out_shape=(jax.ShapeDtypeStruct((4, RANK),...  2.23 us

profile of v4, /device:TPU:1, one launch (start us, length us, event | category | flops | bytes accessed | tf_op | source)
XLA Modules:
  0.0 54.5 jit_solution(15606881434560421742)
XLA Ops:
  0.6 51.6 %plane_and_line_sums.1 = (f32[16,8,128]{2,1,0:T(8,128)S(1)}, bf16[256,896]{1,0:T(8,128)(2,1)S(1)}, f32[128,896]{1,0:T(8,128)S(1)}, f32[32,128]{1,0:T(8,128)S(1)}) custom-call(f32[1,128,896]{2,1,0:T(8,128)} %g_hbm.1, bf16[1,128,896]{2,1,0:T(8,128)(2,1)} %e_hbm.1, f32[32,896]{1,0:T(8,128)} %bitcast.2), custom_call_target="tpu_custom_call" | custom-call | tf_op jit(solution)/shard_map/plane_and_line_sums/pallas_call | solution.py:321
  52.2 2.2 %factors.1 = (f32[4,32]{1,0:T(4,128)}, f32[32,896]{1,0:T(8,128)}, bf16[1,128,896]{2,1,0:T(8,128)(2,1)}) custom-call(f32[16,8,128]{2,1,0:T(8,128)S(1)} %get-tuple-element.10.m_ref, bf16[256,896]{1,0:T(8,128)(2,1)S(1)} %get-tuple-element.11.s_ref, f32[128,896]{1,0:T(8,128)S(1)} %get-tuple-element.12.c_ref, f32[32,128]{1,0:T(8,128)S(1)} %get-tuple-element.13.first_ref), custom_call_target="tpu_custom_call" | custom-call | tf_op jit(solution)/shard_map/factors/pallas_call | solution.py:433

commit v5 on v4

--- a/solution.py
+++ b/solution.py
@@ -26,7 +26,7 @@
 P_STRIDE = 5
 REPLICAS = 32
 BLOCK = 16
-STEPS = (0, 256, 512, 896)
+STEPS = (0, 896)
 VMEM_LIMIT = (64 << 20) - (1120 << 10)
 
 
@@ -126,9 +126,7 @@
         corrected = g_v[:, cols] + e_v[:, cols].astype(jnp.float32)
         c_out[:, cols] = corrected
         ct[cols, :] = corrected.T
-
-    def left_terms():
-        p_part[...] = dot(qt_v[...], ct[...], 1, 0).reshape(P_TILES, 8, ROWS)
+    p_part[...] = dot(qt_v[...], ct[...], 1, 0).reshape(P_TILES, 8, ROWS)
 
     @pl.when(core == 0)
     def _():
@@ -137,8 +135,14 @@
 
     @pl.when(core == 1)
     def _():
-        left_terms()
         pl.semaphore_wait(go_sem, 1)
+
+    for t in range(P_TILES):
+        target = 2 * P_STRIDE * t + 1
+
+        @pl.when(dp != target)
+        def _():
+            send(p_part.at[t], p_tiles.at[dp], pt_sem, (target, z))
 
     mine = core * HALF
     other = (1 - core) * HALF
@@ -149,17 +153,6 @@
         send_sem=swap_sem.at[0], recv_sem=swap_sem.at[1], device_id=(sibling, z), device_id_type=MESH,
     )
     swap.start()
-
-    @pl.when(core == 0)
-    def _():
-        left_terms()
-
-    for t in range(P_TILES):
-        target = 2 * P_STRIDE * t + 1
-
-        @pl.when(dp != target)
-        def _():
-            send(p_part.at[t], p_tiles.at[dp], pt_sem, (target, z))
 
     swap.wait_recv()
     ct[pl.ds(pl.multiple_of(mine, 8), HALF), :] += sib[...]
@@ -273,16 +266,6 @@
 
     first_out[...] = orthonormal_rows(p_v[...].reshape(RANK, ROWS))
 
-    @pl.when(core == 0)
-    def _():
-        wait_bytes(m_out, m_sem.at[1])
-
-    @pl.when(core == 1)
-    def _():
-        wait_bytes(m_out.at[pl.ds(0, CHIPS - 1)], m_sem.at[1])
-        wait_bytes(zb.at[pl.ds(0, DEPTH - 1)], z_sem.at[0])
-        wait_bytes(zb.at[pl.ds(0, PLANE - 1)], m_sem.at[0])
-
     swap.wait_send()
 
     @pl.when(holds_p)
@@ -312,6 +295,19 @@
     @pl.when(chip >= OWNERS)
     def _():
         wait_bytes(ct.at[pl.ds(0, HALF)], rs_sem.at[0])
+
+    @pl.when(core == 1)
+    def _():
+        wait_bytes(zb.at[pl.ds(0, DEPTH - 1)], z_sem.at[0])
+        wait_bytes(zb.at[pl.ds(0, PLANE - 1)], m_sem.at[0])
+
+    @pl.when(core == 0)
+    def _():
+        wait_bytes(m_out, m_sem.at[1])
+
+    @pl.when(core == 1)
+    def _():
+        wait_bytes(m_out.at[pl.ds(0, CHIPS - 1)], m_sem.at[1])
 
 
 def reduce_call(gradients, error_memory, qt_start):

time: 54.6 us -> 54.5 us (level)
  no operation moved by 1% of the time
where the time goes in v5:
time: 54.5 us; the launch traced here: 54.3 us
  Pallas kernels  53.7 us (99%)
  between operations  0.64 us (1%)
    pallas_call x1, Pallas kernels, reduce_call(): pl.pallas_call(reduce_kernel, out_shape=(pltpu.VMEM((CHIPS, 8, ROWS), jnp...  51.6 us
    pallas_call x1, Pallas kernels, factor_call(): pl.pallas_call(factor_kernel, out_shape=(jax.ShapeDtypeStruct((4, RANK),...  2.08 us

profile of v5, /device:TPU:1, one launch (start us, length us, event | category | flops | bytes accessed | tf_op | source)
XLA Modules:
  0.0 54.3 jit_solution(9420161978070606846)
XLA Ops:
  0.6 51.6 %plane_and_line_sums.1 = (f32[16,8,128]{2,1,0:T(8,128)S(1)}, bf16[256,896]{1,0:T(8,128)(2,1)S(1)}, f32[128,896]{1,0:T(8,128)S(1)}, f32[32,128]{1,0:T(8,128)S(1)}) custom-call(f32[1,128,896]{2,1,0:T(8,128)} %g_hbm.1, bf16[1,128,896]{2,1,0:T(8,128)(2,1)} %e_hbm.1, f32[32,896]{1,0:T(8,128)} %bitcast.2), custom_call_target="tpu_custom_call" | custom-call | tf_op jit(solution)/shard_map/plane_and_line_sums/pallas_call | solution.py:317
  52.2 2.1 %factors.1 = (f32[4,32]{1,0:T(4,128)}, f32[32,896]{1,0:T(8,128)}, bf16[1,128,896]{2,1,0:T(8,128)(2,1)}) custom-call(f32[16,8,128]{2,1,0:T(8,128)S(1)} %get-tuple-element.10.m_ref, bf16[256,896]{1,0:T(8,128)(2,1)S(1)} %get-tuple-element.11.s_ref, f32[128,896]{1,0:T(8,128)S(1)} %get-tuple-element.12.c_ref, f32[32,128]{1,0:T(8,128)S(1)} %get-tuple-element.13.first_ref), custom_call_target="tpu_custom_call" | custom-call | tf_op jit(solution)/shard_map/factors/pallas_call | solution.py:429

commit v6 on v4

--- a/solution.py
+++ b/solution.py
@@ -26,7 +26,7 @@
 P_STRIDE = 5
 REPLICAS = 32
 BLOCK = 16
-STEPS = (0, 256, 512, 896)
+STEPS = (0, 896)
 VMEM_LIMIT = (64 << 20) - (1120 << 10)
 
 

time: 54.6 us -> 54.5 us (level)
  no operation moved by 1% of the time
where the time goes in v6:
time: 54.5 us; the launch traced here: 54.3 us
  Pallas kernels  53.7 us (99%)
  between operations  0.64 us (1%)
    pallas_call x1, Pallas kernels, reduce_call(): pl.pallas_call(reduce_kernel, out_shape=(pltpu.VMEM((CHIPS, 8, ROWS), jnp...  51.6 us
    pallas_call x1, Pallas kernels, factor_call(): pl.pallas_call(factor_kernel, out_shape=(jax.ShapeDtypeStruct((4, RANK),...  2.08 us

profile of v6, /device:TPU:1, one launch (start us, length us, event | category | flops | bytes accessed | tf_op | source)
XLA Modules:
  0.0 54.3 jit_solution(10146896706806031336)
XLA Ops:
  0.6 51.6 %plane_and_line_sums.1 = (f32[16,8,128]{2,1,0:T(8,128)S(1)}, bf16[256,896]{1,0:T(8,128)(2,1)S(1)}, f32[128,896]{1,0:T(8,128)S(1)}, f32[32,128]{1,0:T(8,128)S(1)}) custom-call(f32[1,128,896]{2,1,0:T(8,128)} %g_hbm.1, bf16[1,128,896]{2,1,0:T(8,128)(2,1)} %e_hbm.1, f32[32,896]{1,0:T(8,128)} %bitcast.2), custom_call_target="tpu_custom_call" | custom-call | tf_op jit(solution)/shard_map/plane_and_line_sums/pallas_call | solution.py:321
  52.2 2.1 %factors.1 = (f32[4,32]{1,0:T(4,128)}, f32[32,896]{1,0:T(8,128)}, bf16[1,128,896]{2,1,0:T(8,128)(2,1)}) custom-call(f32[16,8,128]{2,1,0:T(8,128)S(1)} %get-tuple-element.10.m_ref, bf16[256,896]{1,0:T(8,128)(2,1)S(1)} %get-tuple-element.11.s_ref, f32[128,896]{1,0:T(8,128)S(1)} %get-tuple-element.12.c_ref, f32[32,128]{1,0:T(8,128)S(1)} %get-tuple-element.13.first_ref), custom_call_target="tpu_custom_call" | custom-call | tf_op jit(solution)/shard_map/factors/pallas_call | solution.py:433
